TPU v7x, 32 devices: a whole 2x2x4 slice. The times are simulated.
32 devices in a mesh: pool: 2 (over y), inst: 4 (over z), tp: 4 (over x, core).
Axes of the slice: x: 2, y: 2, z: 4, core: 2. Of those that a mesh axis runs over, the one named last changes fastest.
Arguments:
- prefill_q: bfloat16 [8, 768, 8, 1024], P(('pool', 'inst'), None, 'tp'), parts along dimension 0, may hold values from -8 to 8
- prefill_kv: bfloat16 [8, 2, 768, 8, 128], P(('pool', 'inst'), None, None, 'tp'), parts along dimension 0, may hold values from -8 to 8
- span_len: int32 [8], P(('pool', 'inst')), parts along dimension 0, may hold values from 1 to 768, as said below
- page_seg: int32 [8, 24], P(('pool', 'inst')), parts along dimension 0, may hold values from 0 to 12, as said below
- page_dest: int32 [8, 24, 1], P(('pool', 'inst')), parts along dimension 0, may hold values from 0 to 3, as said below
- page_row: int32 [8, 24], P(('pool', 'inst')), parts along dimension 0, may hold values from 0 to 15, as said below
- dec_q: bfloat16 [8, 16, 2, 8, 1024], P(('pool', 'inst'), None, None, 'tp'), parts along dimension 0, may hold values from -8 to 8
- dec_new: bfloat16 [8, 16, 2, 2, 8, 128], P(('pool', 'inst'), None, None, None, 'tp'), parts along dimension 0, may hold values from -6 to 6
- cache_kv: bfloat16 [8, 64, 2, 32, 8, 128], P(('pool', 'inst'), None, None, None, 'tp'), parts along dimension 0, may hold values from -8 to 8
- block_table: int32 [8, 64], P(('pool', 'inst')), parts along dimension 0, may hold values from 0 to 63, each once within a row
- cache_len: int32 [8, 16], P(('pool', 'inst')), parts along dimension 0, may hold values from 2 to 128, as said below
Outputs:
- prefill_out: bfloat16 [8, 768, 8, 1024], P(('pool', 'inst'), None, 'tp'), parts along dimension 0
- dec_out: bfloat16 [8, 16, 2, 8, 1024], P(('pool', 'inst'), None, None, 'tp'), parts along dimension 0
There are 2 independent parts, one for each index of `pool`. A program takes and returns all parts, laid end to end along the dimension named above; each array names one. Nothing has to cross between parts.
Inputs may be any that keep to these rules, and one draw needn't show every extreme that they name: `span_len`: some instance's block is full. `page_seg`: never falls along a block, starts at 0 and rises by one from request to request; each request holds 1 to 12 whole pages, and the first request of every block exactly 12. `page_dest`: all pages of one request go to one decode instance; from one instance at most 12 pages go to one decode instance, and exactly that many in every instance. `page_row`: all pages of one request join one row. `block_table`: each instance's row holds each of its pool pages once. `cache_len`: some row holds 128 tokens.
All inputs are finite; a program needn't handle non-finite values.
Results may differ from a plain program's by a relative error of at most 0.0033.
Values may be sent and summed in bfloat16 or wider, within the bound.
No kernel may reach another device: no remote copies, remote signals or barrier semaphores. Data moves between devices by JAX's collectives and lax.ppermute only.
A program may use at most 128 MiB of HBM per device.

v0:
```python
import jax
import jax.numpy as jnp
from jax import lax
from jax.sharding import PartitionSpec as P

NEGATIVE = -1e30
PRECISE = lax.Precision.HIGHEST


def combine(first, second):
    first_top, first_total, first_acc = first
    second_top, second_total, second_acc = second
    joined = jnp.maximum(first_top, second_top)
    first_factor = jnp.exp(first_top - joined)
    second_factor = jnp.exp(second_top - joined)
    return (
        joined,
        first_total * first_factor + second_total * second_factor,
        first_acc * first_factor[..., None] + second_acc * second_factor[..., None],
    )


def prefill_span(queries, keys_vals, length, segments):
    span_size, head_count, row_width = queries.shape
    head_dim = keys_vals.shape[-1]
    groups = row_width // head_dim
    scaling = head_dim ** (-0.5)
    page_size = span_size // segments.shape[0]
    query_sets = queries.reshape(span_size, head_count * groups, head_dim).transpose(1, 0, 2)
    key_sets = keys_vals[0].transpose(1, 0, 2)
    value_sets = keys_vals[1].transpose(1, 0, 2)
    positions = jnp.arange(span_size, dtype=jnp.int32)
    token_seg = jnp.repeat(segments, page_size)
    allowed = (positions[None, :] <= positions[:, None]) & (positions[None, :] < length)
    allowed = allowed & (token_seg[None, :] == token_seg[:, None])

    def attend(item_index):
        head_index = item_index // groups
        scores = (
            lax.dot_general(
                query_sets[item_index],
                key_sets[head_index],
                (((1,), (1,)), ((), ())),
                preferred_element_type=jnp.float32,
            )
            * scaling
        )
        scores = jnp.where(allowed, scores, NEGATIVE)
        row_top = jnp.max(scores, -1, keepdims=True)
        weights_f = jnp.exp(scores - row_top)
        totals = jnp.sum(weights_f, -1, keepdims=True)
        blended = jnp.dot(
            weights_f.astype(jnp.bfloat16),
            value_sets[head_index],
            preferred_element_type=jnp.float32,
        )
        return blended / totals

    results = lax.map(attend, jnp.arange(head_count * groups, dtype=jnp.int32))
    results = jnp.where((positions < length)[None, :, None], results, 0.0)
    return results.transpose(1, 0, 2).reshape(span_size, head_count, row_width).astype(jnp.bfloat16)


def cache_partial(queries, pool, table, lengths):
    row_count = table.shape[0]
    pages = jnp.take(pool, table, axis=0)
    pages = jnp.swapaxes(pages, 1, 2).reshape(row_count, 2, -1, pool.shape[3], pool.shape[4])
    scaling = pool.shape[-1] ** (-0.5)
    scores = (
        jnp.einsum("bshgd,bthd->bshgt", queries, pages[:, 0], preferred_element_type=jnp.float32)
        * scaling
    )
    token_ids = jnp.arange(pages.shape[2], dtype=jnp.int32)
    allowed = (token_ids[None, :] < lengths[:, None])[:, None, None, None, :]
    scores = jnp.where(allowed, scores, NEGATIVE)
    row_top = jnp.max(scores, -1)
    weights_f = jnp.where(allowed, jnp.exp(scores - row_top[..., None]), 0.0)
    blended = jnp.einsum(
        "bshgt,bthd->bshgd", weights_f, pages[:, 1].astype(jnp.float32), precision=PRECISE
    )
    return (row_top, jnp.sum(weights_f, -1), blended)


def fresh_partial(queries, fresh):
    scaling = fresh.shape[-1] ** (-0.5)
    scores = (
        jnp.einsum("bshgd,bthd->bshgt", queries, fresh[:, :, 0], preferred_element_type=jnp.float32)
        * scaling
    )
    step_ids = jnp.arange(fresh.shape[1], dtype=jnp.int32)
    allowed = (step_ids[None, :] <= step_ids[:, None])[None, :, None, None, :]
    scores = jnp.where(allowed, scores, NEGATIVE)
    row_top = jnp.max(scores, -1)
    weights_f = jnp.where(allowed, jnp.exp(scores - row_top[..., None]), 0.0)
    blended = jnp.einsum(
        "bshgt,bthd->bshgd", weights_f, fresh[:, :, 1].astype(jnp.float32), precision=PRECISE
    )
    return (row_top, jnp.sum(weights_f, -1), blended)


def page_partial(queries, page_keys, page_values, row_tag, counts):
    row_count = queries.shape[0]
    page_size = page_keys.shape[1]
    scaling = page_keys.shape[-1] ** (-0.5)
    safe_tag = jnp.maximum(row_tag, 0)
    picked = jnp.take(queries, safe_tag, axis=0)
    scores = (
        jnp.einsum("rshgd,rthd->rshgt", picked, page_keys, preferred_element_type=jnp.float32)
        * scaling
    )
    token_ids = jnp.arange(page_size, dtype=jnp.int32)
    allowed = (token_ids[None, :] < counts[:, None]) & (row_tag >= 0)[:, None]
    allowed = allowed[:, None, None, None, :]
    scores = jnp.where(allowed, scores, NEGATIVE)
    page_top = jnp.max(scores, -1)
    member = row_tag[None, :] == jnp.arange(row_count, dtype=jnp.int32)[:, None]
    row_top = jnp.max(jnp.where(member[:, :, None, None, None], page_top[None], NEGATIVE), axis=1)
    weights_f = jnp.where(
        allowed, jnp.exp(scores - jnp.take(row_top, safe_tag, axis=0)[..., None]), 0.0
    )
    member_f = member.astype(jnp.float32)
    totals = jnp.einsum("br,rshg->bshg", member_f, jnp.sum(weights_f, -1), precision=PRECISE)
    blended = jnp.einsum(
        "rshgt,rthd->rshgd", weights_f, page_values.astype(jnp.float32), precision=PRECISE
    )
    blended = jnp.einsum("br,rshgd->bshgd", member_f, blended, precision=PRECISE)
    return (row_top, totals, blended)


def split_pages(keys_vals, lengths, page_size):
    sources, _, span_size, head_count, head_dim = keys_vals.shape
    per_span = span_size // page_size
    page_keys = keys_vals[:, 0].reshape(sources * per_span, page_size, head_count, head_dim)
    page_values = keys_vals[:, 1].reshape(sources * per_span, page_size, head_count, head_dim)
    starts = jnp.arange(per_span, dtype=jnp.int32) * page_size
    counts = jnp.clip(lengths[:, None] - starts[None, :], 0, page_size).reshape(-1)
    return (page_keys, page_values, counts)


def shards(
    prefill_q,
    prefill_kv,
    span_len,
    page_seg,
    page_dest,
    page_row,
    dec_q,
    dec_new,
    cache_kv,
    block_table,
    cache_len,
):
    my_index = lax.axis_index("inst")
    length = span_len[0]
    prefill_out = prefill_span(prefill_q[0], prefill_kv[0], length, page_seg[0])[None]
    row_count, step_count, head_count, row_width = dec_q.shape[1:]
    head_dim = prefill_kv.shape[-1]
    page_size = cache_kv.shape[3]
    queries = dec_q[0].reshape(row_count, step_count, head_count, row_width // head_dim, head_dim)
    table = block_table[0].reshape(row_count, -1)
    state = combine(
        cache_partial(queries, cache_kv[0], table, cache_len[0]), fresh_partial(queries, dec_new[0])
    )
    kv_portion = lax.all_gather(prefill_kv, "inst", axis=0, tiled=True)
    len_portion = lax.all_gather(span_len, "inst", axis=0, tiled=True)
    dest_portion = lax.all_gather(page_dest, "inst", axis=0, tiled=True)
    row_portion = lax.all_gather(page_row, "inst", axis=0, tiled=True)
    page_keys, page_values, counts = split_pages(kv_portion, len_portion, page_size)
    row_tag = jnp.where(dest_portion[:, :, 0] == my_index, row_portion, -1).reshape(-1)
    state = combine(state, page_partial(queries, page_keys, page_values, row_tag, counts))
    row_top, totals, blended = state
    dec_out = (blended / totals[..., None]).reshape(row_count, step_count, head_count, row_width)
    return (prefill_out, dec_out.astype(jnp.bfloat16)[None])


def solution(mesh):
    return jax.shard_map(
        shards,
        mesh=mesh,
        in_specs=(
            P(("pool", "inst"), None, "tp", None),
            P(("pool", "inst"), None, None, "tp", None),
            P(("pool", "inst")),
            P(("pool", "inst"), None),
            P(("pool", "inst"), None, None),
            P(("pool", "inst"), None),
            P(("pool", "inst"), None, None, "tp", None),
            P(("pool", "inst"), None, None, None, "tp", None),
            P(("pool", "inst"), None, None, None, "tp", None),
            P(("pool", "inst"), None),
            P(("pool", "inst"), None),
        ),
        out_specs=(
            P(("pool", "inst"), None, "tp", None),
            P(("pool", "inst"), None, None, "tp", None),
        ),
        check_vma=False,
    )
```

profile of v0, /device:TPU:0, one launch (start us, length us, event | category | flops | bytes accessed | tf_op | source)
XLA Modules:
  0.0 224.8 jit_solution(14315114838332422733)
XLA Ops:
  7.2 2.3 %copy.133 = bf16[1,2,768,2,128]{4,2,0,3,1:T(8,128)(2,1)} copy(bf16[1,2,768,2,128]{4,3,2,1,0:T(2,128)(2,1)} %param.14) | data formatting | bytes 1572864 | tf_op args[1]
  10.9 8.7 %copy.118 = bf16[1,768,2,1024]{1,3,2,0:T(8,128)(2,1)} copy(bf16[1,768,2,1024]{3,2,1,0:T(2,128)(2,1)} %param.13) | data formatting | bytes 6291456 | tf_op args[0]
  22.6 120.2 %while.14 = (s32[]{:T(128)}, bf16[16,768,128]{2,1,0:T(8,128)(2,1)}, s32[16]{0:T(128)S(1)}, bf16[16,768,128]{1,2,0:T(8,128)(2,1)}, bf16[2,768,128]{2,1,0:T(8,128)...) while((s32[]{:T(128)}, bf16[16,768,128]{2,1,0:T(8,128)(2,1)}, ...), condition=%wide.region_3.4_spmd.clone.clone, body=%wide.region_0.3_spmd.clone.sunk.clone | while | flops 308574720 | bytes 8087882 | solution.py:59
  26.9 1.6 fusion.86
  34.4 1.6 fusion.86
  72.0 1.6 fusion.86
  94.5 1.6 fusion.86
  102.0 1.6 fusion.86
  117.0 1.6 fusion.86
  124.5 1.6 fusion.86
  139.6 1.6 fusion.86
  142.8 9.9 %all-reduce = s32[4]{0:T(128)S(1)} all-reduce(s32[4]{0:T(128)S(1)} %dynamic-update-slice), channel_id=1, replica_groups=mesh['pool'=2,'inst'=4,'tp'=4] {'inst'}, use_global_device_ids=true, to_apply=%add | all-reduce | flops 4 | bytes 32
  152.7 2.8 %fusion.18 = bf16[768,16,128]{2,0,1:T(8,128)(2,1)S(1)} fusion(bf16[16,768,128]{2,1,0:T(8,128)(2,1)} %get-tuple-element.92, pred[768]{0:T(1024)(128)(4,1)S(1)} %get-tuple-element.301), kind=kLoop, calls=%fused_computation.24 | loop fusion | flops 1572864 | bytes 6292224 | tf_op jit(solution)/shard_map/convert_element_type | solution.py:61
  155.5 3.7 %copy.122 = bf16[768,16,128]{2,1,0:T(8,128)(2,1)} copy(bf16[768,16,128]{2,0,1:T(8,128)(2,1)S(1)} %fusion.18) | data formatting | bytes 6291456 | tf_op jit(solution)/shard_map/convert_element_type | solution.py:61
  159.2 5.5 %convert_element_type.41 = bf16[1,768,2,1024]{3,2,1,0:T(2,128)(2,1)} reshape(bf16[768,16,128]{2,1,0:T(8,128)(2,1)} %copy.122) | data formatting | bytes 6291456 | tf_op jit(solution)/shard_map/convert_element_type | solution.py:61
  164.9 9.1 %all-gather = s32[4,1,24]{2,1,0:T(1,128)S(1)} all-gather(s32[1,1,24]{2,1,0:T(1,128)S(1)} %bitcast.163), channel_id=1, replica_groups=mesh['pool'=2,'inst'=4,'tp'=4] {'inst'}, dimensions={0}, use_global_device_ids=true | all-gather | bytes 480 | tf_op jit(solution)/shard_map/all_gather | solution.py:167
  174.0 7.9 %all_gather.12 = s32[4,24,1]{1,2,0:T(1,128)S(1)} all-gather(s32[1,24,1]{1,2,0:T(1,128)S(1)} %copy-done.25), channel_id=1, replica_groups=mesh['pool'=2,'inst'=4,'tp'=4] {'inst'}, dimensions={0}, use_global_device_ids=true | all-gather | bytes 480 | tf_op jit(solution)/shard_map/all_gather | solution.py:166
  186.2 6.9 %gather_fusion = bf16[64,2,32,2,128]{4,3,2,1,0:T(2,128)(2,1)} fusion(bf16[64,2,32,2,128]{4,3,2,1,0:T(2,128)(2,1)S(1)} %bitcast.150, s32[1024]{0:T(1024)S(1)} %pad_clamp_fusion.1), kind=kCustom, calls=%fused_computation | custom fusion | bytes 4194560 | tf_op jit(solution)/shard_map/jit(_take)/gather | solution.py:66
  193.2 1.9 copy_select_fusion
  198.3 3.4 %fusion.69 = (bf16[4,1,768,2,128]{4,2,0,3,1:T(8,128)(2,1)}, bf16[4,1,768,2,128]{4,2,0,3,1:T(8,128)(2,1)S(1)}) fusion(bf16[4,2,768,2,128]{4,2,0,3,1:T(8,128)(2,1)} %all-gather.3.cloned.1.call-done), kind=kLoop, calls=%fused_computation.111 | loop fusion | bytes 6291456 | tf_op jit(solution)/shard_map/slice | solution.py:134
  201.7 2.3 %bitcast_reduce_fusion = (f32[96,2,2,8]{3,1,2,0:T(2,128)S(1)}, f32[96,2,2,8,32]{4,3,2,1,0:T(8,128)}) fusion(bf16[96,32,2,128,1]{3,1,0,2,4:T(8,128)(2,1)S(1)} %bitcast.156, pred[96,32]{1,0:T(8,128)(4,1)S(1)} %fusion.55, bf16[96,2,2,8,128]{4,3,2,1,0:T(8,128)(2,1)S(1)} %gather_fusion.1, pred[96]{0:T(512)(128)(4,1)S(1)} %get-tuple-element.185), kind=kOutput, calls=%fused_computation.29 | convolution fusion | flops 25850880 | bytes 2767968 | tf_op jit(solution)/shard_map/rshgd,rthd->rshgt/dot_general | solution.py:108
  206.2 2.4 %fusion.32 = f32[96,2,2,8]{3,1,2,0:T(2,128)S(1)} fusion(f32[96,2,2,8,32]{4,3,2,1,0:T(8,128)} %get-tuple-element.187, f32[96,2,2,8]{3,1,2,0:T(2,128)S(1)} %copy.140, pred[96,32]{1,0:T(8,128)(4,1)} %copy-done.10), kind=kLoop, calls=%fused_computation.38 | loop fusion | flops 291840 | bytes 420864 | tf_op jit(solution)/shard_map/reduce_sum | solution.py:122
  209.6 3.5 %fusion.27 = f32[96,2,2,8,128]{4,3,1,2,0:T(8,128)S(1)} fusion(bf16[96,32,2,128,1]{3,1,0,2,4:T(8,128)(2,1)} %bitcast.155, f32[96,2,2,8,32]{4,3,2,1,0:T(8,128)} %get-tuple-element.187, f32[96,2,2,8]{3,1,2,0:T(2,128)S(1)} %copy.140, pred[96,32]{1,0:T(8,128)(4,1)S(1)} %copy-done.11), kind=kOutput, calls=%fused_computation.37 | convolution fusion | flops 151191552 | bytes 3554304 | tf_op jit(solution)/shard_map/rshgt,rthd->rshgd/dot_general | solution.py:123
  215.0 2.2 fusion.42
  (177 shorter events, 64.7 us)
Async XLA Ops:
  7.2 179.0 %copy-start = (bf16[1,64,2,32,2,128]{5,4,3,2,1,0:T(2,128)(2,1)S(1)}, bf16[1,64,2,32,2,128]{5,4,3,2,1,0:T(2,128)(2,1)}, u32[]{:S(2)}) copy-start(bf16[1,64,2,32,2,128]{5,4,3,2,1,0:T(2,128)(2,1)} %param.21) | copy-start | bytes 6291460
  7.2 191.1 %all-gather.3.cloned.1.call-start = ((), (), s32[]{:S(2)}) async-start(), calls=%async_computation | async-start | bytes 3932160 | tf_op jit(solution)/shard_map/all_gather | solution.py:164
  10.9 9.4 %copy-start.23 = (s32[1,24]{1,0:T(1,128)S(1)}, s32[1,24]{1,0:T(1,128)}, u32[]{:S(2)}) copy-start(s32[1,24]{1,0:T(1,128)} %param.16) | copy-start | bytes 292
  10.9 9.5 %copy-start.3 = (bf16[1,1,768,2,128]{4,3,2,1,0:T(2,128)(2,1)S(1)}, bf16[1,1,768,2,128]{4,3,2,1,0:T(2,128)(2,1)}, u32[]{:S(2)}) copy-start(bf16[1,1,768,2,128]{4,3,2,1,0:T(2,128)(2,1)} %get-tuple-element.183) | copy-start | bytes 1179652
  10.9 10.4 %copy-start.28 = (u32[32]{0:T(128)S(1)}, u32[32]{0:T(128)}, u32[]{:S(2)}) copy-start(u32[32]{0:T(128)} %constant.152) | copy-start | bytes 388
  159.2 5.7 %copy-start.24 = (s32[1,24]{1,0:T(1,128)S(1)}, s32[1,24]{1,0:T(1,128)}, u32[]{:S(2)}) copy-start(s32[1,24]{1,0:T(1,128)} %param.18) | copy-start | bytes 292
  159.2 14.8 %copy-start.25 = (s32[1,24,1]{1,2,0:T(1,128)S(1)}, s32[1,24,1]{1,2,0:T(1,128)}, u32[]{:S(2)}) copy-start(s32[1,24,1]{1,2,0:T(1,128)} %param.17) | copy-start | bytes 292
  159.2 22.8 %copy-start.4 = (bf16[1,16,2,2,1024]{4,3,2,1,0:T(2,128)(2,1)S(1)}, bf16[1,16,2,2,1024]{4,3,2,1,0:T(2,128)(2,1)}, u32[]{:S(2)}) copy-start(bf16[1,16,2,2,1024]{4,3,2,1,0:T(2,128)(2,1)} %param.19) | copy-start | bytes 393220
  159.2 23.0 %copy-start.12 = (bf16[1,16,2,2,2,128]{5,4,3,2,1,0:T(2,128)(2,1)S(1)}, bf16[1,16,2,2,2,128]{5,4,3,2,1,0:T(2,128)(2,1)}, u32[]{:S(2)}) copy-start(bf16[1,16,2,2,2,128]{5,4,3,2,1,0:T(2,128)(2,1)} %param.20) | copy-start | bytes 98308
  164.8 20.0 %copy-start.26 = (s32[1,64]{1,0:T(1,128)S(1)}, s32[1,64]{1,0:T(1,128)}, u32[]{:S(2)}) copy-start(s32[1,64]{1,0:T(1,128)} %param.22) | copy-start | bytes 772
  182.0 16.1 %copy-start.17 = (s32[96]{0:T(128)}, s32[96]{0:T(128)S(1)}, u32[]{:S(2)}) copy-start(s32[96]{0:T(128)S(1)} %eq.50) | copy-start | bytes 1156
  183.0 10.1 %copy-start.20 = (pred[2,2]{1,0:T(4,128)(4,1)}, pred[2,2]{1,0:T(4,128)(4,1)S(1)}, u32[]{:S(2)}) copy-start(pred[2,2]{1,0:T(4,128)(4,1)S(1)} %iota_compare_fusion.7) | copy-start | bytes 16
  183.7 9.4 %copy-start.5 = (f32[16,2,2,8,2]{3,4,1,2,0:T(2,128)}, f32[16,2,2,8,2]{3,4,1,2,0:T(2,128)S(1)}, u32[]{:S(2)}) copy-start(f32[16,2,2,8,2]{3,4,1,2,0:T(2,128)S(1)} %get-tuple-element.189) | copy-start | bytes 12292
  186.2 7.0 %copy-start.27 = (s32[1,16]{1,0:T(1,128)S(1)}, s32[1,16]{1,0:T(1,128)}, u32[]{:S(2)}) copy-start(s32[1,16]{1,0:T(1,128)} %param.23) | copy-start | bytes 196
  193.2 4.0 %copy-start.15 = (pred[16,128]{1,0:T(8,128)(4,1)}, pred[16,128]{1,0:T(8,128)(4,1)S(1)}, u32[]{:S(2)}) copy-start(pred[16,128]{1,0:T(8,128)(4,1)S(1)} %iota_compare_fusion.3) | copy-start | bytes 6148
  198.2 3.5 %copy-start.22 = (pred[96]{0:T(512)(128)(4,1)}, pred[96]{0:T(512)(128)(4,1)S(1)}, u32[]{:S(2)}) copy-start(pred[96]{0:T(512)(128)(4,1)S(1)} %get-tuple-element.185) | copy-start | bytes 292
  204.0 4.8 %copy-start.18 = (s32[96]{0:T(128)S(1)}, s32[96]{0:T(128)}, u32[]{:S(2)}) copy-start(s32[96]{0:T(128)} %copy-done.17) | copy-start | bytes 1156
  204.0 4.9 %copy-start.7 = (f32[16,2,2,8]{0,3,2,1:T(8,128)S(1)}, f32[16,2,2,8]{0,3,2,1:T(8,128)}, u32[]{:S(2)}) copy-start(f32[16,2,2,8]{0,3,2,1:T(8,128)} %copy.147) | copy-start | bytes 6148
  204.0 4.9 %copy-start.8 = (f32[16,2,2,8]{0,3,2,1:T(8,128)S(1)}, f32[16,2,2,8]{0,3,2,1:T(8,128)}, u32[]{:S(2)}) copy-start(f32[16,2,2,8]{0,3,2,1:T(8,128)} %copy.129) | copy-start | bytes 6148
  204.0 4.9 %copy-start.9 = (f32[16,2,2,8]{0,3,2,1:T(8,128)S(1)}, f32[16,2,2,8]{0,3,2,1:T(8,128)}, u32[]{:S(2)}) copy-start(f32[16,2,2,8]{0,3,2,1:T(8,128)} %copy.146) | copy-start | bytes 6148
  204.0 5.1 %copy-start.6 = (f32[16,2,2,8,2]{3,4,1,2,0:T(2,128)S(1)}, f32[16,2,2,8,2]{3,4,1,2,0:T(2,128)}, u32[]{:S(2)}) copy-start(f32[16,2,2,8,2]{3,4,1,2,0:T(2,128)} %copy-done.5) | copy-start | bytes 12292
  204.0 5.1 %copy-start.14 = (bf16[1,16,2,2,2,128]{5,2,4,1,3,0:T(2,128)(2,1)S(1)}, bf16[1,16,2,2,2,128]{5,2,4,1,3,0:T(2,128)(2,1)}, u32[]{:S(2)}) copy-start(bf16[1,16,2,2,2,128]{5,2,4,1,3,0:T(2,128)(2,1)} %copy-done.13) | copy-start | bytes 98308
  204.0 5.1 %copy-start.21 = (pred[2,2]{1,0:T(4,128)(4,1)S(1)}, pred[2,2]{1,0:T(4,128)(4,1)}, u32[]{:S(2)}) copy-start(pred[2,2]{1,0:T(4,128)(4,1)} %copy-done.20) | copy-start | bytes 16
  209.6 5.4 %copy-start.16 = (pred[16,128]{1,0:T(8,128)(4,1)S(1)}, pred[16,128]{1,0:T(8,128)(4,1)}, u32[]{:S(2)}) copy-start(pred[16,128]{1,0:T(8,128)(4,1)} %copy-done.15) | copy-start | bytes 6148
  (6 other events, 12.8 us)
Sparse Core Ops, SparseCore 0:
  9.7 66.1 all-gather.2
where the time goes:
time: 227 us; the launch traced here: 225 us
  loops' own time  59.5 us (26%)
  matrix products  56.9 us (25%)
  local copies, waits for them, and re-layouts  50.8 us (22%)
  blocking collectives  26.9 us (12%)
  other arithmetic  15.5 us (7%)
  between operations  15.2 us (7%)
    another operation x1, loops' own time, prefill_span(): results = lax.map(attend, jnp.arange(head_count * groups, dtype=jnp.int32))  59.5 us
    dot_general x16, matrix products, attend(): lax.dot_general(query_sets[item_index], key_sets[head_index], (((1,), (1,...  25.9 us
    dot_general x16, matrix products, attend(): jnp.dot(weights_f.astype(jnp.bfloat16), value_sets[head_index], preferred...  19.5 us
    unnamed x66, local copies, waits for them, and re-layouts  14.4 us
    unnamed x1, blocking collectives  9.92 us
    dynamic_slice x16, local copies, waits for them, and re-layouts, prefill_span(): results = lax.map(attend, jnp.arange(head_count * groups, dtype=jnp.int32))  9.41 us
    convert_element_type x2, local copies, waits for them, and re-layouts, prefill_span(): results.transpose(1, 0, 2).reshape(span_size, head_count, row_width)  9.24 us
    all_gather x1, blocking collectives, shards(): row_portion = lax.all_gather(page_row, 'inst', axis=0, tiled=True)  9.1 us
  transfers between devices with their start and end apart: 1, of which 0 were waited for; matrix products, arithmetic and copies ran while one was open for 45% of the time, Pallas kernels for 0%

commit v1 on v0

v1 whole, which is shorter than its diff:
```python
import functools
import math

import jax
import jax.numpy as jnp
from jax import lax
from jax.experimental import pallas as pl
from jax.experimental.pallas import tpu as pltpu
from jax.sharding import PartitionSpec as P

NEGATIVE = -1e30
LOG2E = math.log2(math.e)
LANES = 128
DIRECT = 8
VMEM_LIMIT = 48 * 1024 * 1024

SMEM_SPEC = pl.BlockSpec(memory_space=pltpu.SMEM)
VMEM_SPEC = pl.BlockSpec(memory_space=pltpu.VMEM)


def query_rows(field):
    lead = math.prod(field.shape[:-2])
    heads, width = field.shape[-2:]
    split = field.reshape(lead, heads, width // LANES, LANES)
    return split.transpose(0, 2, 1, 3).reshape(-1, LANES)


def from_rows(rows, shape):
    heads, width = shape[-2:]
    lead = math.prod(shape[:-2])
    split = rows.reshape(lead, width // LANES, heads, LANES)
    return split.transpose(0, 2, 1, 3).reshape(shape)


def head_of(shape, axis, heads):
    return lax.broadcasted_iota(jnp.int32, shape, axis) % heads


def dot_nt(first, second):
    return lax.dot_general(
        first, second, (((1,), (1,)), ((), ())), preferred_element_type=jnp.float32
    )


def dot_nn(first, second):
    return jnp.dot(first, second, preferred_element_type=jnp.float32)


def two_terms(weights):
    upper = weights.astype(jnp.bfloat16)
    lower = (weights - upper.astype(jnp.float32)).astype(jnp.bfloat16)
    return jnp.concatenate([upper, lower], axis=0)


def spread_heads(rows, heads):
    if heads == 1:
        return rows
    owner = head_of(rows.shape, 0, heads)
    zero = jnp.zeros_like(rows)
    return jnp.concatenate([jnp.where(owner == h, rows, zero) for h in range(heads)], axis=1)


def pick_head(wide, heads):
    if heads == 1:
        return wide
    owner = head_of((wide.shape[0], LANES), 0, heads)
    picked = wide[:, :LANES]
    for h in range(1, heads):
        picked = jnp.where(owner == h, wide[:, h * LANES : (h + 1) * LANES], picked)
    return picked


def cache_kernel(
    sizes, seg_ref, dest_ref, row_ref, len_ref, table_ref, clen_ref,
    q_ref, fresh_ref, pool_ref, kv_ref,
    info_ref, part_ref, lse_ref, keys_ref, vals_ref,
    scr_ref, fscr_ref,
):
    heads, page, pages, rows, steps, pages_max, requests = sizes
    span = pages * page
    length = len_ref[0]

    for r in range(info_ref.shape[1]):
        for f in range(4):
            info_ref[f, r] = 0

    def note(p, _):
        r = seg_ref[0, p]
        fresh_request = jnp.logical_or(p == 0, r != seg_ref[0, jnp.maximum(p - 1, 0)])

        @pl.when(fresh_request)
        def _():
            info_ref[0, r] = p * page
            info_ref[2, r] = dest_ref[0, p]
            info_ref[3, r] = row_ref[0, p]

        info_ref[1, r] = jnp.minimum((p + 1) * page, length)
        return 0

    lax.fori_loop(0, pages, note, 0)

    for part, out_ref in enumerate((keys_ref, vals_ref)):
        if heads == 1:
            out_ref[...] = kv_ref[part * span : (part + 1) * span, :]
        else:
            scr_ref[...] = kv_ref[part * span * heads : (part + 1) * span * heads, :].astype(
                jnp.float32
            )
            for h in range(heads):
                out_ref[:, h * LANES : (h + 1) * LANES] = scr_ref[
                    pl.ds(h, span, stride=heads), :
                ].astype(jnp.bfloat16)

    scale2 = LANES**-0.5 * LOG2E
    per_row = q_ref.shape[0] // rows
    groups = per_row // (steps * heads)
    fresh_rows = fresh_ref.shape[0]
    fscr_ref[...] = jnp.zeros_like(fscr_ref)
    fscr_ref[:fresh_rows, :] = fresh_ref[...]
    fresh = fscr_ref[...]
    width = fresh.shape[0]
    page_rows = page * heads

    col = lax.broadcasted_iota(jnp.int32, (per_row, width), 1)
    sub = lax.broadcasted_iota(jnp.int32, (per_row, width), 0)
    fresh_ok = (
        ((col // heads) % 2 == 0)
        & ((col // (2 * heads)) % steps <= sub // (groups * heads))
        & (col % heads == sub % heads)
    )
    col_row = col // (2 * heads * steps)
    ccol = lax.broadcasted_iota(jnp.int32, (per_row, pages_max * page_rows), 1)
    csub = lax.broadcasted_iota(jnp.int32, (per_row, pages_max * page_rows), 0)
    same_head = ccol % heads == csub % heads
    ctok = ccol // heads

    for b in range(rows):
        q_b = q_ref[b * per_row : (b + 1) * per_row, :]
        tables = [table_ref[0, b * pages_max + j] for j in range(pages_max)]

        def gather(part):
            pieces = [
                pool_ref[
                    pl.ds(pl.multiple_of((t * 2 + part) * page_rows, page_rows), page_rows), :
                ]
                for t in tables
            ]
            return jnp.concatenate(pieces, axis=0)

        s_c = dot_nt(q_b, gather(0))
        s_f = dot_nt(q_b, fresh)
        keep_c = same_head & (ctok < clen_ref[0, b])
        keep_f = fresh_ok & (col_row == b)
        s_c = jnp.where(keep_c, s_c, NEGATIVE)
        s_f = jnp.where(keep_f, s_f, NEGATIVE)
        top = jnp.maximum(
            jnp.max(s_c, axis=1, keepdims=True), jnp.max(s_f, axis=1, keepdims=True)
        )
        w_c = jnp.where(keep_c, jnp.exp2((s_c - top) * scale2), 0.0)
        w_f = jnp.where(keep_f, jnp.exp2((s_f - top) * scale2), 0.0)
        total = jnp.sum(w_c, axis=1, keepdims=True) + jnp.sum(w_f, axis=1, keepdims=True)
        acc = dot_nn(two_terms(w_c), gather(1))
        acc = acc + dot_nn(two_terms(pltpu.roll(w_f, heads, 1)), fresh)
        blended = acc[:per_row] + acc[per_row:]
        part_ref[b * per_row : (b + 1) * per_row, :] = blended / total
        lse = top * scale2 + jnp.log2(total)
        lse_ref[b * per_row : (b + 1) * per_row, :] = jnp.broadcast_to(lse, (per_row, LANES))


def pages_kernel(sizes, per_slot, info_ref, *refs):
    heads, page, pages, rows, steps, pages_max, requests, instances = sizes
    slot_count = instances // per_slot
    slots = refs[:slot_count]
    keys_ref, vals_ref, own_ref, send_ref, q_scr = refs[slot_count:]
    me = lax.axis_index("inst")
    per_row = slots[0].shape[0] // (per_slot * rows)
    span = pages * page
    scale2 = LANES**-0.5 * LOG2E
    for r in range(requests):
        slot = lax.rem(me - info_ref[2, r] + instances, instances)
        row = info_ref[3, r]
        if slot_count == 1:
            start = pl.multiple_of((slot * rows + row) * per_row, per_row)
            q_scr[r * per_row : (r + 1) * per_row, :] = slots[0][pl.ds(start, per_row), :]
        else:
            start = pl.multiple_of(row * per_row, per_row)
            for k in range(slot_count):

                @pl.when(slot == k)
                def _():
                    q_scr[r * per_row : (r + 1) * per_row, :] = slots[k][pl.ds(start, per_row), :]

    scores = dot_nt(spread_heads(q_scr[...], heads), keys_ref[...])
    token = lax.broadcasted_iota(jnp.int32, (per_row, span), 1)
    weights, tops, totals = [], [], []
    for r in range(requests):
        keep = (token >= info_ref[0, r]) & (token < info_ref[1, r])
        s_r = jnp.where(keep, scores[r * per_row : (r + 1) * per_row], NEGATIVE)
        top = jnp.max(s_r, axis=1, keepdims=True)
        w_r = jnp.where(keep, jnp.exp2((s_r - top) * scale2), 0.0)
        weights.append(w_r)
        tops.append(top)
        totals.append(jnp.sum(w_r, axis=1, keepdims=True))
    count = requests * per_row
    acc = dot_nn(two_terms(jnp.concatenate(weights, axis=0)), vals_ref[...])
    acc = pick_head(acc[:count] + acc[count:], heads)
    total = jnp.concatenate(totals, axis=0)
    live = total > 0.0
    blended = jnp.where(live, acc / jnp.where(live, total, 1.0), 0.0)
    lse = jnp.where(
        live,
        jnp.concatenate(tops, axis=0) * scale2 + jnp.log2(jnp.where(live, total, 1.0)),
        NEGATIVE,
    )
    own_ref[...] = blended
    send_ref[:count, :] = blended.astype(jnp.bfloat16)
    blocks = -(-count // LANES)
    lines = []
    for j in range(blocks):
        piece = lse[j * LANES : min((j + 1) * LANES, count)]
        shape = (piece.shape[0], LANES)
        same = lax.broadcasted_iota(jnp.int32, shape, 0) == lax.broadcasted_iota(
            jnp.int32, shape, 1
        )
        lines.append(jnp.sum(jnp.where(same, piece, 0.0), axis=0, keepdims=True))
    line = jnp.concatenate(lines, axis=0)
    first = line.astype(jnp.bfloat16)
    rest = line - first.astype(jnp.float32)
    second = rest.astype(jnp.bfloat16)
    third = (rest - second.astype(jnp.float32)).astype(jnp.bfloat16)
    spare = send_ref.shape[0] - count
    terms = [t.astype(jnp.float32) for t in (first, second, third)]
    terms.append(jnp.zeros((spare - 3 * blocks, LANES), jnp.float32))
    send_ref[count:, :] = jnp.concatenate(terms, axis=0).astype(jnp.bfloat16)


def prefill_kernel(sizes, seg_ref, info_ref, len_ref, q_ref, keys_ref, vals_ref, after_ref, out_ref, lag_ref):
    heads, page, pages, block = sizes
    tile = pl.program_id(0)
    page_rows = out_ref.shape[0] * page // block
    per_token = page_rows // page
    per_block = block // page
    scale2 = LANES**-0.5 * LOG2E
    length = len_ref[0]

    @pl.when(tile == 0)
    def _():
        lane = lax.broadcasted_iota(jnp.int32, lag_ref.shape, 1)
        lag_ref[...] = lane - lax.broadcasted_iota(jnp.int32, lag_ref.shape, 0) // per_token

    first_key = info_ref[0, seg_ref[0, tile * per_block]]
    first_block = first_key // block
    behind = tile - first_block

    def attend(count):
        base = (tile - (count - 1)) * block
        keys = keys_ref[pl.ds(pl.multiple_of(base, block), count * block), :]
        vals = vals_ref[pl.ds(pl.multiple_of(base, block), count * block), :]
        lane = lax.broadcasted_iota(jnp.int32, (1, block), 1)
        for p in range(per_block):
            rows = slice(p * page_rows, (p + 1) * page_rows)
            scores = dot_nt(spread_heads(q_ref[rows, :], heads), keys)
            start = info_ref[0, seg_ref[0, tile * per_block + p]] - base
            pieces = []
            for j in range(count):
                s_j = scores[:, j * block : (j + 1) * block]
                keep = lane >= start - j * block
                if j == count - 1:
                    keep = keep & (lag_ref[...] <= p * page)
                pieces.append(jnp.where(keep, s_j, NEGATIVE))
            top = pieces[0]
            for piece in pieces[1:]:
                top = jnp.maximum(top, piece)
            top = jnp.max(top, axis=1, keepdims=True)
            weights = [jnp.exp2((piece - top) * scale2) for piece in pieces]
            total = weights[0]
            for w_j in weights[1:]:
                total = total + w_j
            total = jnp.sum(total, axis=1, keepdims=True)
            joined = jnp.concatenate([w_j.astype(jnp.bfloat16) for w_j in weights], axis=1)
            acc = pick_head(dot_nn(joined, vals), heads)
            place = lax.broadcasted_iota(jnp.int32, (page_rows, 1), 0) // per_token
            live = place < length - (tile * block + p * page)
            out_ref[rows, :] = (acc * jnp.where(live, 1.0 / total, 0.0)).astype(jnp.bfloat16)

    longest = 3
    for count in range(1, longest + 1):
        pl.when(behind == count - 1)(functools.partial(attend, count))


def join_kernel(sizes, per_slot, *refs):
    heads, rows, requests, instances = sizes
    slot_count = instances // per_slot
    infos = refs[:slot_count]
    own_ref = refs[slot_count]
    sent = refs[slot_count + 1 : 2 * slot_count + 1]
    part_ref, lse_ref, out_ref, top_scr, total_scr, acc_scr = refs[2 * slot_count + 1 :]
    me = lax.axis_index("inst")
    per_row = part_ref.shape[0] // rows
    count = requests * per_row
    blocks = -(-count // LANES)
    top_scr[...] = lse_ref[...]
    total_scr[...] = jnp.ones_like(total_scr)
    acc_scr[...] = part_ref[...]
    lane = lax.broadcasted_iota(jnp.int32, (per_row, LANES), 1)
    sub = lax.broadcasted_iota(jnp.int32, (per_row, LANES), 0)

    def absorb(slot_ref, info_ref, line, index, values_ref):
        for r in range(requests):

            @pl.when(jnp.logical_and(info_ref[index * 4 + 2, r] == me, info_ref[index * 4 + 1, r] > info_ref[index * 4, r]))
            def _():
                place = pl.ds(pl.multiple_of(info_ref[index * 4 + 3, r] * per_row, per_row), per_row)
                j, offset = divmod(r * per_row, LANES)
                spread = jnp.where(lane == sub + offset, line[j : j + 1, :], 0.0)
                level = jnp.sum(spread, axis=1, keepdims=True)
                top = top_scr[place, :]
                joined = jnp.maximum(top, level)
                old = jnp.exp2(top - joined)
                new = jnp.exp2(level - joined)
                values = values_ref(r)
                top_scr[place, :] = joined
                total_scr[place, :] = total_scr[place, :] * old + new
                acc_scr[place, :] = acc_scr[place, :] * old + values * new

    for k in range(slot_count):
        tall = sent[k].shape[0] // per_slot
        for i in range(per_slot):
            base = i * tall
            stats = sent[k][base + count : base + tall, :].astype(jnp.float32)
            line = stats[:blocks] + stats[blocks : 2 * blocks] + stats[2 * blocks : 3 * blocks]

            def values_ref(r, k=k, i=i, base=base):
                if k == 0 and i == 0:
                    return own_ref[r * per_row : (r + 1) * per_row, :]
                spot = base + r * per_row
                return sent[k][spot : spot + per_row, :].astype(jnp.float32)

            absorb(sent[k], infos[k], line, i, values_ref)
    out_ref[...] = (acc_scr[...] / total_scr[...]).astype(jnp.bfloat16)


def exchange(block, instances):
    if instances <= DIRECT:
        slots = [block]
        for k in range(1, instances):
            slots.append(
                lax.ppermute(block, "inst", [(i, (i + k) % instances) for i in range(instances)])
            )
        return slots
    whole = lax.all_gather(block, "inst", axis=0)
    order = lax.rem(lax.axis_index("inst") - jnp.arange(instances) + instances, instances)
    return [jnp.take(whole, order, axis=0).reshape((-1,) + block.shape[1:])]


def params(**extra):
    return pltpu.CompilerParams(vmem_limit_bytes=VMEM_LIMIT, **extra)


def shards(
    instances,
    prefill_q,
    prefill_kv,
    span_len,
    page_seg,
    page_dest,
    page_row,
    dec_q,
    dec_new,
    cache_kv,
    block_table,
    cache_len,
):
    _, span, heads, width = prefill_q.shape
    pages = page_seg.shape[1]
    _, rows, steps = dec_q.shape[:3]
    pool, page = cache_kv.shape[1], cache_kv.shape[3]
    pages_max = block_table.shape[1] // rows
    capacity = -(-2 * pages // instances)
    requests = pages - capacity + 1
    groups = width // LANES
    per_row = steps * groups * heads
    block = LANES
    sizes = (heads, page, pages, rows, steps, pages_max, requests)
    dest = page_dest.reshape(1, pages)
    slot_width = 32
    f32, bf16, i32 = jnp.float32, jnp.bfloat16, jnp.int32
    shape = jax.ShapeDtypeStruct

    queries = query_rows(dec_q[0])
    q_slots = exchange(queries, instances)
    per_slot = instances // len(q_slots)

    info, part, lse, keys, vals = pl.pallas_call(
        functools.partial(cache_kernel, sizes),
        out_shape=(
            shape((4, slot_width), i32),
            shape((rows * per_row, LANES), f32),
            shape((rows * per_row, LANES), f32),
            shape((span, heads * LANES), bf16),
            shape((span, heads * LANES), bf16),
        ),
        in_specs=[SMEM_SPEC] * 6 + [VMEM_SPEC] * 4,
        out_specs=(SMEM_SPEC,) + (VMEM_SPEC,) * 4,
        scratch_shapes=[
            pltpu.VMEM((span * heads, LANES), f32),
            pltpu.VMEM((-(-dec_new[0].size // LANES // LANES) * LANES, LANES), bf16),
        ],
        compiler_params=params(),
        name="cache",
    )(
        page_seg, dest, page_row, span_len, block_table, cache_len,
        queries, dec_new.reshape(-1, LANES), cache_kv.reshape(-1, LANES),
        prefill_kv.reshape(-1, LANES),
    )
    info_slots = exchange(info, instances)

    count = requests * per_row
    tall = count + -(-3 * -(-count // LANES) // 16) * 16
    own, sent = pl.pallas_call(
        functools.partial(pages_kernel, sizes + (instances,), per_slot),
        out_shape=(shape((count, LANES), f32), shape((tall, LANES), bf16)),
        in_specs=[SMEM_SPEC] + [VMEM_SPEC] * (len(q_slots) + 2),
        out_specs=(VMEM_SPEC, VMEM_SPEC),
        scratch_shapes=[pltpu.VMEM((count, LANES), bf16)],
        compiler_params=params(),
        name="pages",
    )(info, *q_slots, keys, vals)
    sent_slots = exchange(sent, instances)

    q_rows = query_rows(prefill_q[0])
    tile_rows = block * groups * heads
    tiles = span // block
    whole = lambda i: (0, 0)
    prefill_out = pl.pallas_call(
        functools.partial(prefill_kernel, (heads, page, pages, block)),
        out_shape=shape(q_rows.shape, bf16),
        grid=(tiles,),
        in_specs=[SMEM_SPEC] * 3
        + [
            pl.BlockSpec((tile_rows, LANES), lambda i: (i, 0)),
            pl.BlockSpec(keys.shape, whole),
            pl.BlockSpec(vals.shape, whole),
            pl.BlockSpec(memory_space=pl.ANY),
        ],
        out_specs=pl.BlockSpec((tile_rows, LANES), lambda i: (i, 0)),
        scratch_shapes=[pltpu.VMEM((page * groups * heads, block), i32)],
        compiler_params=params(),
        name="prefill",
    )(page_seg, info, span_len, q_rows, keys, vals, own)

    dec_out = pl.pallas_call(
        functools.partial(join_kernel, (heads, rows, requests, instances), per_slot),
        out_shape=shape((rows * per_row, LANES), bf16),
        in_specs=[SMEM_SPEC] * len(info_slots) + [VMEM_SPEC] * (3 + len(sent_slots)),
        out_specs=VMEM_SPEC,
        scratch_shapes=[pltpu.VMEM((rows * per_row, LANES), f32)] * 3,
        compiler_params=params(),
        name="join",
    )(*info_slots, own, *sent_slots, part, lse)

    return (
        from_rows(prefill_out, prefill_q.shape),
        from_rows(dec_out, dec_q.shape),
    )


def solution(mesh):
    return jax.shard_map(
        functools.partial(shards, mesh.shape["inst"]),
        mesh=mesh,
        in_specs=(
            P(("pool", "inst"), None, "tp", None),
            P(("pool", "inst"), None, None, "tp", None),
            P(("pool", "inst")),
            P(("pool", "inst"), None),
            P(("pool", "inst"), None, None),
            P(("pool", "inst"), None),
            P(("pool", "inst"), None, None, "tp", None),
            P(("pool", "inst"), None, None, None, "tp", None),
            P(("pool", "inst"), None, None, None, "tp", None),
            P(("pool", "inst"), None),
            P(("pool", "inst"), None),
        ),
        out_specs=(
            P(("pool", "inst"), None, "tp", None),
            P(("pool", "inst"), None, None, "tp", None),
        ),
        check_vma=False,
    )
```

time: 227 us -> 51.8 us (0.23)
  loops' own time: 59.5 us -> 0 us
  matrix products: 56.9 us -> 0 us
  local copies, waits for them, and re-layouts: 50.8 us -> 9.21 us
  blocking collectives: 26.9 us -> 0 us
  Pallas kernels: 0 us -> 21 us
  starting transfers between devices: 0.04 us -> 18.2 us
  other arithmetic: 15.5 us -> 0 us
  between operations: 15.2 us -> 1.38 us
    another operation x1 -> x0, loops' own time: 59.5 us -> none  [prefill_span(): results = lax.map(attend, jnp.arange(head_count * groups, dtype=jnp.int32))]
    dot_general x39 -> x0, matrix products: 56.8 us -> none  [the longest x16 25.9 us: attend(): lax.dot_general(query_sets[item_index], key_sets[head_index], (((1,), (1,...]
    pallas_call x0 -> x4, Pallas kernels: none -> 21 us  [the longest x1 9.93 us: shards(): pl.pallas_call(functools.partial(prefill_kernel, (heads, page, pages, blo...]
    ppermute x0 -> x9, starting transfers between devices: none -> 18.2 us  [exchange(): lax.ppermute(block, 'inst', [(i, (i + k) % instances) for i in range(inst...]
    all_gather x2 -> x0, blocking collectives: 17 us -> none  [the longest x1 9.1 us: shards(): row_portion = lax.all_gather(page_row, 'inst', axis=0, tiled=True)]
    unnamed x1 -> x0, blocking collectives: 9.92 us -> none
    dynamic_slice x16 -> x0, local copies, waits for them, and re-layouts: 9.41 us -> none  [prefill_span(): results = lax.map(attend, jnp.arange(head_count * groups, dtype=jnp.int32))]
    convert_element_type x3 -> x0, local copies, waits for them, and re-layouts: 9.28 us -> none  [the longest x2 9.24 us: prefill_span(): results.transpose(1, 0, 2).reshape(span_size, head_count, row_width)]
  transfers between devices with their start and end apart: 1 -> 9, of which waited for: 0 -> 1; matrix products, arithmetic and copies ran while one was open for 45% -> 0% of each run, Pallas kernels for 0% -> 32%
where the time goes in v1:
time: 51.8 us; the launch traced here: 51.5 us
  Pallas kernels  21 us (41%)
  starting transfers between devices  18.2 us (35%)
  local copies, waits for them, and re-layouts  9.21 us (18%)
  waiting for transfers between devices  1.67 us (3%)
  between operations  1.38 us (3%)
    ppermute x9, starting transfers between devices, exchange(): lax.ppermute(block, 'inst', [(i, (i + k) % instances) for i in range(inst...  18.2 us
    pallas_call x1, Pallas kernels, shards(): pl.pallas_call(functools.partial(prefill_kernel, (heads, page, pages, blo...  9.93 us
    unnamed x24, local copies, waits for them, and re-layouts  9.21 us
    pallas_call x1, Pallas kernels, shards(): pl.pallas_call(functools.partial(cache_kernel, sizes), out_shape=(shape((...  6.69 us
    pallas_call x1, Pallas kernels, shards(): pl.pallas_call(functools.partial(join_kernel, (heads, rows, requests, ins...  2.25 us
    pallas_call x1, Pallas kernels, shards(): pl.pallas_call(functools.partial(pages_kernel, sizes + (instances,), per_...  2.16 us
    ppermute x9, waiting for transfers between devices, exchange(): lax.ppermute(block, 'inst', [(i, (i + k) % instances) for i in range(inst...  1.67 us
  transfers between devices with their start and end apart: 9, of which 1 were waited for; matrix products, arithmetic and copies ran while one was open for 0% of the time, Pallas kernels for 32%

profile of v1, /device:TPU:0, one launch (start us, length us, event | category | flops | bytes accessed | tf_op | source)
XLA Modules:
  0.0 51.5 jit_solution(14579166780922035189)
XLA Ops:
  0.6 5.1 %collective-permute-start.2 = (bf16[512,128]{1,0:T(8,128)(2,1)}, bf16[512,128]{1,0:T(8,128)(2,1)S(1)}, u32[]{:S(2)}, u32[]{:S(2)}) collective-permute-start(bf16[512,128]{1,0:T(8,128)(2,1)} %bitcast.27), channel_id=1, source_target_pairs={{0,12},{4,0},{8,4},{12,8},{1,13},{5,1},{9,5},{13,9},{2,14},{6,2},{... | collective-permute-start | bytes 393224 | tf_op jit(solution)/shard_map/ppermute | solution.py:348
  5.7 1.0 %collective-permute-start = (bf16[512,128]{1,0:T(8,128)(2,1)}, bf16[512,128]{1,0:T(8,128)(2,1)S(1)}, u32[]{:S(2)}, u32[]{:S(2)}) collective-permute-start(bf16[512,128]{1,0:T(8,128)(2,1)} %bitcast.29), channel_id=1, source_target_pairs={{0,4},{4,8},{8,12},{12,0},{1,5},{5,9},{9,13},{13,1},{2,6},{6,10},{... | collective-permute-start | bytes 393224 | tf_op jit(solution)/shard_map/ppermute | solution.py:348
  7.4 1.6 %copy-done.1 = bf16[1,64,2,32,2,128]{5,4,3,2,1,0:T(2,128)(2,1)S(1)} copy-done((bf16[1,64,2,32,2,128]{5,4,3,2,1,0:T(2,128)(2,1)S(1)}, bf16[1,64,2,32,2,128]{5,4,3,2,1,0:T(2,128)(2,1)}, u32[]{:S(2)}) %copy-start.1) | copy-done | bytes 2097176
  9.0 1.1 %copy-done.2 = bf16[1,2,768,2,128]{4,3,2,1,0:T(2,128)(2,1)S(1)} copy-done((bf16[1,2,768,2,128]{4,3,2,1,0:T(2,128)(2,1)S(1)}, bf16[1,2,768,2,128]{4,3,2,1,0:T(2,128)(2,1)}, u32[]{:S(2)}) %copy-start.2) | copy-done | bytes 786456
  10.1 0.9 %copy-done.3 = bf16[1,16,2,2,1024]{4,3,2,1,0:T(2,128)(2,1)S(1)} copy-done((bf16[1,16,2,2,1024]{4,3,2,1,0:T(2,128)(2,1)S(1)}, bf16[1,16,2,2,1024]{4,3,2,1,0:T(2,128)(2,1)}, u32[]{:S(2)}) %copy-start.3) | copy-done | bytes 131096
  11.0 0.8 %copy-done.5 = bf16[1,16,2,2,2,128]{5,4,3,2,1,0:T(2,128)(2,1)S(1)} copy-done((bf16[1,16,2,2,2,128]{5,4,3,2,1,0:T(2,128)(2,1)S(1)}, bf16[1,16,2,2,2,128]{5,4,3,2,1,0:T(2,128)(2,1)}, u32[]{:S(2)}) %copy-start.5) | copy-done | bytes 32792
  11.8 0.7 %copy-done.6 = s32[1,24]{1,0:T(1,128)S(1)} copy-done((s32[1,24]{1,0:T(1,128)S(1)}, s32[1,24]{1,0:T(1,128)}, u32[]{:S(2)}) %copy-start.6) | copy-done | bytes 120
  12.5 0.7 %copy-done.8 = s32[1,24,1]{1,2,0:T(1,128)S(1)} copy-done((s32[1,24,1]{1,2,0:T(1,128)S(1)}, s32[1,24,1]{1,2,0:T(1,128)}, u32[]{:S(2)}) %copy-start.8) | copy-done | bytes 120
  13.1 0.7 %copy-done.9 = s32[1,24]{1,0:T(1,128)S(1)} copy-done((s32[1,24]{1,0:T(1,128)S(1)}, s32[1,24]{1,0:T(1,128)}, u32[]{:S(2)}) %copy-start.9) | copy-done | bytes 120
  13.8 0.7 %copy-done.10 = s32[1,64]{1,0:T(1,128)S(1)} copy-done((s32[1,64]{1,0:T(1,128)S(1)}, s32[1,64]{1,0:T(1,128)}, u32[]{:S(2)}) %copy-start.10) | copy-done | bytes 280
  14.4 0.7 %copy-done.11 = s32[1,16]{1,0:T(1,128)S(1)} copy-done((s32[1,16]{1,0:T(1,128)S(1)}, s32[1,16]{1,0:T(1,128)}, u32[]{:S(2)}) %copy-start.11) | copy-done | bytes 88
  15.1 6.7 %cache.1 = (s32[4,32]{1,0:T(4,128)S(1)}, f32[512,128]{1,0:T(8,128)S(1)}, f32[512,128]{1,0:T(8,128)S(1)}, bf16[768,256]{1,0:T(8,128)(2,1)S(1)}, bf16[768,256]{1,0:T(8,128)(2,1)S(1)}) custom-call(s32[1,24]{1,0:T(1,128)S(1)} %copy-done.6, s32[1,24]{1,0:T(1,128)S(1)} %bitcast.33, s32[1,24]{1,0:T(1,128)S(1)} %copy-done.9, s32[1]{0:T(128)S(6)} %copy.17.len_ref, ...), custom_call_target="tpu_custom_call" | custom-call | tf_op jit(solution)/shard_map/cache/pallas_call | solution.py:394
  21.8 0.0 collective-permute-done.1.refs_2_
  21.8 0.0 copy-start.4
  21.8 0.9 %copy-done.4 = bf16[1,16,2,2,1024]{4,3,2,1,0:T(2,128)(2,1)S(1)} copy-done((bf16[1,16,2,2,1024]{4,3,2,1,0:T(2,128)(2,1)S(1)}, bf16[1,16,2,2,1024]{4,3,2,1,0:T(2,128)(2,1)}, u32[]{:S(2)}) %copy-start.4) | copy-done | bytes 131096
  22.7 2.2 %pages.1 = (f32[416,128]{1,0:T(8,128)S(1)}, bf16[432,128]{1,0:T(8,128)(2,1)S(1)}) custom-call(s32[4,32]{1,0:T(4,128)S(1)} %get-tuple-element.9.info_ref.refs_0_, bf16[512,128]{1,0:T(8,128)(2,1)S(1)} %bitcast.31, bf16[512,128]{1,0:T(8,128)(2,1)S(1)} %collective-permute-done.refs_1_, bf16[512,128]{1,0:T(8,128)(2,1)S(1)} %collective-permute-done.1.refs_2_, ...), custom_call_target="tpu_custom_call" | custom-call | tf_op jit(solution)/shard_map/pages/pallas_call | solution.py:420
  24.9 2.9 %collective-permute-start.8 = (bf16[432,128]{1,0:T(8,128)(2,1)S(1)}, bf16[432,128]{1,0:T(8,128)(2,1)S(1)}, u32[]{:S(2)}, u32[]{:S(2)}) collective-permute-start(bf16[432,128]{1,0:T(8,128)(2,1)S(1)} %get-tuple-element.13.refs_5_), channel_id=1, source_target_pairs={{0,12},{4,0},{8,4},{12,8},{1,13},{5,1},{9,5},{13,9},{2,14},{6,2},{... | collective-permute-start | bytes 331784 | tf_op jit(solution)/shard_map/ppermute | solution.py:348
  27.7 1.1 %collective-permute-start.7 = (bf16[432,128]{1,0:T(8,128)(2,1)S(1)}, bf16[432,128]{1,0:T(8,128)(2,1)S(1)}, u32[]{:S(2)}, u32[]{:S(2)}) collective-permute-start(bf16[432,128]{1,0:T(8,128)(2,1)S(1)} %get-tuple-element.13.refs_5_), channel_id=1, source_target_pairs={{0,8},{4,12},{8,0},{12,4},{1,9},{5,13},{9,1},{13,5},{2,10},{6,14},... | collective-permute-start | bytes 331784 | tf_op jit(solution)/shard_map/ppermute | solution.py:348
  28.9 3.8 %collective-permute-start.5 = (s32[4,32]{1,0:T(4,128)S(1)}, s32[4,32]{1,0:T(4,128)S(1)}, u32[]{:S(2)}, u32[]{:S(2)}) collective-permute-start(s32[4,32]{1,0:T(4,128)S(1)} %get-tuple-element.9.info_ref.refs_0_), channel_id=1, source_target_pairs={{0,12},{4,0},{8,4},{12,8},{1,13},{5,1},{9,5},{13,9},{2,14},{6,2},{... | collective-permute-start | bytes 1544 | tf_op jit(solution)/shard_map/ppermute | solution.py:348
  32.7 1.7 %collective-permute-done.5.refs_3_ = s32[4,32]{1,0:T(4,128)S(1)} collective-permute-done((s32[4,32]{1,0:T(4,128)S(1)}, s32[4,32]{1,0:T(4,128)S(1)}, u32[]{:S(2)}, u32[]{:S(2)}) %collective-permute-start.5) | collective-permute-done | bytes 544 | tf_op jit(solution)/shard_map/ppermute | solution.py:348
  34.4 4.3 %collective-permute-start.3 = (s32[4,32]{1,0:T(4,128)S(1)}, s32[4,32]{1,0:T(4,128)S(1)}, u32[]{:S(2)}, u32[]{:S(2)}) collective-permute-start(s32[4,32]{1,0:T(4,128)S(1)} %get-tuple-element.9.info_ref.refs_0_), channel_id=1, source_target_pairs={{0,4},{4,8},{8,12},{12,0},{1,5},{5,9},{9,13},{13,1},{2,6},{6,10},{... | collective-permute-start | bytes 1544 | tf_op jit(solution)/shard_map/ppermute | solution.py:348
  38.6 0.7 %copy-done.7 = s32[1,24]{1,0:T(1,128)S(1)} copy-done((s32[1,24]{1,0:T(1,128)S(1)}, s32[1,24]{1,0:T(1,128)}, u32[]{:S(2)}) %copy-start.7) | copy-done | bytes 120
  39.3 9.9 %prefill.1 = bf16[12288,128]{1,0:T(8,128)(2,1)} custom-call(s32[1,24]{1,0:T(1,128)S(1)} %copy-done.7, s32[4,32]{1,0:T(4,128)S(1)} %get-tuple-element.9.info_ref.refs_0_, s32[1]{0:T(128)S(6)} %copy.17.len_ref, bf16[12288,128]{1,0:T(8,128)(2,1)S(1)} %bitcast.24, bf16[768,256]{1,0:T(8,128)(2,1)S(1)} %get-tuple-element.10.refs_4_.keys_ref, ...), custom_call_target="tpu_custom_call" | custom-call | tf_op jit(solution)/shard_map/prefill/pallas_call | solution.py:435
  49.3 2.2 %join.1 = bf16[512,128]{1,0:T(8,128)(2,1)} custom-call(s32[4,32]{1,0:T(4,128)S(1)} %get-tuple-element.9.info_ref.refs_0_, s32[4,32]{1,0:T(4,128)S(1)} %collective-permute-done.3.refs_1_, s32[4,32]{1,0:T(4,128)S(1)} %collective-permute-done.4.refs_2_, s32[4,32]{1,0:T(4,128)S(1)} %collective-permute-done.5.refs_3_, ...), custom_call_target="tpu_custom_call" | custom-call | tf_op jit(solution)/shard_map/join/pallas_call | solution.py:452
  (22 shorter events, 0.0 us)
Async XLA Ops:
  0.6 38.0 %copy-start = (bf16[1,768,2,1024]{3,2,1,0:T(2,128)(2,1)S(1)}, bf16[1,768,2,1024]{3,2,1,0:T(2,128)(2,1)}, u32[]{:S(2)}) copy-start(bf16[1,768,2,1024]{3,2,1,0:T(2,128)(2,1)} %param.11) | copy-start | bytes 9437188
  0.6 21.1 %collective-permute-start.2 = (bf16[512,128]{1,0:T(8,128)(2,1)}, bf16[512,128]{1,0:T(8,128)(2,1)S(1)}, u32[]{:S(2)}, u32[]{:S(2)}) collective-permute-start(bf16[512,128]{1,0:T(8,128)(2,1)} %bitcast.27), channel_id=1, source_target_pairs={{0,12},{4,0},{8,4},{12,8},{1,13},{5,1},{9,5},{13,9},{2,14},{6,2},{... | collective-permute-start | bytes 393224 | tf_op jit(solution)/shard_map/ppermute | solution.py:348
  5.7 16.0 %collective-permute-start.1 = (bf16[512,128]{1,0:T(8,128)(2,1)}, bf16[512,128]{1,0:T(8,128)(2,1)S(1)}, u32[]{:S(2)}, u32[]{:S(2)}) collective-permute-start(bf16[512,128]{1,0:T(8,128)(2,1)} %bitcast.28), channel_id=1, source_target_pairs={{0,8},{4,12},{8,0},{12,4},{1,9},{5,13},{9,1},{13,5},{2,10},{6,14},... | collective-permute-start | bytes 393224 | tf_op jit(solution)/shard_map/ppermute | solution.py:348
  5.7 16.1 %collective-permute-start = (bf16[512,128]{1,0:T(8,128)(2,1)}, bf16[512,128]{1,0:T(8,128)(2,1)S(1)}, u32[]{:S(2)}, u32[]{:S(2)}) collective-permute-start(bf16[512,128]{1,0:T(8,128)(2,1)} %bitcast.29), channel_id=1, source_target_pairs={{0,4},{4,8},{8,12},{12,0},{1,5},{5,9},{9,13},{13,1},{2,6},{6,10},{... | collective-permute-start | bytes 393224 | tf_op jit(solution)/shard_map/ppermute | solution.py:348
  7.4 1.6 %copy-start.1 = (bf16[1,64,2,32,2,128]{5,4,3,2,1,0:T(2,128)(2,1)S(1)}, bf16[1,64,2,32,2,128]{5,4,3,2,1,0:T(2,128)(2,1)}, u32[]{:S(2)}) copy-start(bf16[1,64,2,32,2,128]{5,4,3,2,1,0:T(2,128)(2,1)} %param.19) | copy-start | bytes 6291460
  9.0 1.1 %copy-start.2 = (bf16[1,2,768,2,128]{4,3,2,1,0:T(2,128)(2,1)S(1)}, bf16[1,2,768,2,128]{4,3,2,1,0:T(2,128)(2,1)}, u32[]{:S(2)}) copy-start(bf16[1,2,768,2,128]{4,3,2,1,0:T(2,128)(2,1)} %param.12) | copy-start | bytes 2359300
  10.1 0.9 %copy-start.3 = (bf16[1,16,2,2,1024]{4,3,2,1,0:T(2,128)(2,1)S(1)}, bf16[1,16,2,2,1024]{4,3,2,1,0:T(2,128)(2,1)}, u32[]{:S(2)}) copy-start(bf16[1,16,2,2,1024]{4,3,2,1,0:T(2,128)(2,1)} %param.17) | copy-start | bytes 393220
  11.0 0.8 %copy-start.5 = (bf16[1,16,2,2,2,128]{5,4,3,2,1,0:T(2,128)(2,1)S(1)}, bf16[1,16,2,2,2,128]{5,4,3,2,1,0:T(2,128)(2,1)}, u32[]{:S(2)}) copy-start(bf16[1,16,2,2,2,128]{5,4,3,2,1,0:T(2,128)(2,1)} %param.18) | copy-start | bytes 98308
  11.8 0.7 %copy-start.6 = (s32[1,24]{1,0:T(1,128)S(1)}, s32[1,24]{1,0:T(1,128)}, u32[]{:S(2)}) copy-start(s32[1,24]{1,0:T(1,128)} %seg_ref.3) | copy-start | bytes 292
  12.5 0.7 %copy-start.8 = (s32[1,24,1]{1,2,0:T(1,128)S(1)}, s32[1,24,1]{1,2,0:T(1,128)}, u32[]{:S(2)}) copy-start(s32[1,24,1]{1,2,0:T(1,128)} %param.15) | copy-start | bytes 292
  13.1 0.7 %copy-start.9 = (s32[1,24]{1,0:T(1,128)S(1)}, s32[1,24]{1,0:T(1,128)}, u32[]{:S(2)}) copy-start(s32[1,24]{1,0:T(1,128)} %row_ref.1) | copy-start | bytes 292
  13.8 0.7 %copy-start.10 = (s32[1,64]{1,0:T(1,128)S(1)}, s32[1,64]{1,0:T(1,128)}, u32[]{:S(2)}) copy-start(s32[1,64]{1,0:T(1,128)} %table_ref.1) | copy-start | bytes 772
  14.4 0.7 %copy-start.11 = (s32[1,16]{1,0:T(1,128)S(1)}, s32[1,16]{1,0:T(1,128)}, u32[]{:S(2)}) copy-start(s32[1,16]{1,0:T(1,128)} %clen_ref.1) | copy-start | bytes 196
  21.8 0.9 %copy-start.4 = (bf16[1,16,2,2,1024]{4,3,2,1,0:T(2,128)(2,1)S(1)}, bf16[1,16,2,2,1024]{4,3,2,1,0:T(2,128)(2,1)}, u32[]{:S(2)}) copy-start(bf16[1,16,2,2,1024]{4,3,2,1,0:T(2,128)(2,1)} %param.17) | copy-start | bytes 393220
  24.9 24.4 %collective-permute-start.8 = (bf16[432,128]{1,0:T(8,128)(2,1)S(1)}, bf16[432,128]{1,0:T(8,128)(2,1)S(1)}, u32[]{:S(2)}, u32[]{:S(2)}) collective-permute-start(bf16[432,128]{1,0:T(8,128)(2,1)S(1)} %get-tuple-element.13.refs_5_), channel_id=1, source_target_pairs={{0,12},{4,0},{8,4},{12,8},{1,13},{5,1},{9,5},{13,9},{2,14},{6,2},{... | collective-permute-start | bytes 331784 | tf_op jit(solution)/shard_map/ppermute | solution.py:348
  27.7 21.5 %collective-permute-start.7 = (bf16[432,128]{1,0:T(8,128)(2,1)S(1)}, bf16[432,128]{1,0:T(8,128)(2,1)S(1)}, u32[]{:S(2)}, u32[]{:S(2)}) collective-permute-start(bf16[432,128]{1,0:T(8,128)(2,1)S(1)} %get-tuple-element.13.refs_5_), channel_id=1, source_target_pairs={{0,8},{4,12},{8,0},{12,4},{1,9},{5,13},{9,1},{13,5},{2,10},{6,14},... | collective-permute-start | bytes 331784 | tf_op jit(solution)/shard_map/ppermute | solution.py:348
  28.9 20.4 %collective-permute-start.6 = (bf16[432,128]{1,0:T(8,128)(2,1)S(1)}, bf16[432,128]{1,0:T(8,128)(2,1)S(1)}, u32[]{:S(2)}, u32[]{:S(2)}) collective-permute-start(bf16[432,128]{1,0:T(8,128)(2,1)S(1)} %get-tuple-element.13.refs_5_), channel_id=1, source_target_pairs={{0,4},{4,8},{8,12},{12,0},{1,5},{5,9},{9,13},{13,1},{2,6},{6,10},{... | collective-permute-start | bytes 331784 | tf_op jit(solution)/shard_map/ppermute | solution.py:348
  28.9 5.5 %collective-permute-start.5 = (s32[4,32]{1,0:T(4,128)S(1)}, s32[4,32]{1,0:T(4,128)S(1)}, u32[]{:S(2)}, u32[]{:S(2)}) collective-permute-start(s32[4,32]{1,0:T(4,128)S(1)} %get-tuple-element.9.info_ref.refs_0_), channel_id=1, source_target_pairs={{0,12},{4,0},{8,4},{12,8},{1,13},{5,1},{9,5},{13,9},{2,14},{6,2},{... | collective-permute-start | bytes 1544 | tf_op jit(solution)/shard_map/ppermute | solution.py:348
  32.7 16.5 %collective-permute-start.4 = (s32[4,32]{1,0:T(4,128)S(1)}, s32[4,32]{1,0:T(4,128)S(1)}, u32[]{:S(2)}, u32[]{:S(2)}) collective-permute-start(s32[4,32]{1,0:T(4,128)S(1)} %get-tuple-element.9.info_ref.refs_0_), channel_id=1, source_target_pairs={{0,8},{4,12},{8,0},{12,4},{1,9},{5,13},{9,1},{13,5},{2,10},{6,14},... | collective-permute-start | bytes 1544 | tf_op jit(solution)/shard_map/ppermute | solution.py:348
  34.4 14.9 %collective-permute-start.3 = (s32[4,32]{1,0:T(4,128)S(1)}, s32[4,32]{1,0:T(4,128)S(1)}, u32[]{:S(2)}, u32[]{:S(2)}) collective-permute-start(s32[4,32]{1,0:T(4,128)S(1)} %get-tuple-element.9.info_ref.refs_0_), channel_id=1, source_target_pairs={{0,4},{4,8},{8,12},{12,0},{1,5},{5,9},{9,13},{13,1},{2,6},{6,10},{... | collective-permute-start | bytes 1544 | tf_op jit(solution)/shard_map/ppermute | solution.py:348
  38.6 0.7 %copy-start.7 = (s32[1,24]{1,0:T(1,128)S(1)}, s32[1,24]{1,0:T(1,128)}, u32[]{:S(2)}) copy-start(s32[1,24]{1,0:T(1,128)} %seg_ref.3) | copy-start | bytes 292
